TPU v7x, 32 devices: a whole 2x2x4 slice. The times are simulated.
32 devices in a mesh: rep: 2 (over x), dp: 16 (over z, y, core).
Axes of the slice: x: 2, y: 2, z: 4, core: 2. Of those that a mesh axis runs over, the one named last changes fastest.
Arguments:
- queries: bfloat16 [12288, 6144], P(('rep', 'dp')), parts along dimension 0, may hold values from -48 to 48
- latents: bfloat16 [12288, 576], P(('rep', 'dp')), parts along dimension 0, may hold values from -48 to 48
- kv_weight: bfloat16 [512, 6144], replicated, may hold values from -1 to 1
- lengths: int32 [192], P('rep'), parts along dimension 0, may hold values from 1 to 128, 6144 in all
Outputs:
- attn_out: bfloat16 [12288, 2048], P(('rep', 'dp')), parts along dimension 0
- hessian: float32 [4096, 2048], P(('rep', 'dp')), parts along dimension 0
There are 2 independent parts, one for each index of `rep`. A program takes and returns all parts, laid end to end along the dimension named above; an argument that names none is the same for every part. Nothing has to cross between parts.
Inputs may be any that keep to these rules, and one draw needn't show every extreme that they name: lengths of the 96 traces packed end to end in order; they sum to 6144 and the largest is exactly 128.
All inputs are finite; a program needn't handle non-finite values.
Results may differ from a plain program's by a relative error of at most 0.0065.
Values may be sent and summed in bfloat16 or wider, within the bound.
A program may use at most 128 MiB of HBM per device.

v0:
```python
import math

import jax
import jax.numpy as jnp
from jax import lax
from jax.sharding import PartitionSpec as P

HEADS = 32
NOPE = 128
ROPE = 64
V_DIM = 64
KV_RANK = 512
MAXLEN = 128
OUT_WIDTH = 2048


MASKED = -1e30
block_rows = 128


def passed_along(value, axis, steps):
    count = lax.axis_size(axis)
    initial, last = (max(0, -steps), min(count, count - steps))
    return lax.ppermute(value, axis, [(source, source + steps) for source in range(initial, last)])


def per_device(queries, latents, kv_weight, lengths):
    devices = lax.axis_size("dp")
    device = lax.axis_index("dp")
    local_rows = queries.shape[0]
    all_tokens = local_rows * devices
    score_scale = 1.0 / math.sqrt(NOPE + ROPE)
    head_width = NOPE + V_DIM
    count = min(local_rows, MAXLEN)
    earlier_parts = [passed_along(latents[local_rows - count :], "dp", 1)]
    window_latent = jnp.concatenate(earlier_parts + [latents], axis=0)
    window_kv = jnp.dot(
        window_latent[:, :KV_RANK], kv_weight, preferred_element_type=jnp.float32
    ).astype(jnp.bfloat16)
    window_rope = window_latent[:, KV_RANK:]
    window_kv = window_kv.reshape(local_rows + MAXLEN, HEADS, head_width)
    trace_ends = jnp.cumsum(lengths)
    first_row = device * local_rows
    query_pos = first_row + jnp.arange(local_rows, dtype=jnp.int32)
    key_pos = first_row - MAXLEN + jnp.arange(local_rows + MAXLEN, dtype=jnp.int32)
    query_trace = jnp.searchsorted(trace_ends, query_pos, side="right")
    key_trace = jnp.searchsorted(trace_ends, key_pos, side="right")
    allowed = (
        (query_trace[:, None] == key_trace[None, :])
        & (key_pos[None, :] <= query_pos[:, None])
        & (key_pos[None, :] >= 0)
    )
    query_heads = queries.reshape(local_rows, HEADS, NOPE + ROPE)
    query_span = min(block_rows, local_rows)
    key_span = query_span + MAXLEN
    outputs = []
    for block_first in range(0, local_rows, query_span):
        kv_part = window_kv[block_first : block_first + key_span]
        rope_part = window_rope[block_first : block_first + key_span]
        keys_full = jnp.concatenate(
            [
                kv_part[:, :, :NOPE],
                jnp.broadcast_to(rope_part[:, None, :], (key_span, HEADS, ROPE)),
            ],
            axis=2,
        )
        query_part = query_heads[block_first : block_first + query_span]
        scores = jnp.einsum(
            "qhd,khd->hqk", query_part, keys_full, preferred_element_type=jnp.float32
        )
        block_mask = allowed[
            block_first : block_first + query_span, block_first : block_first + key_span
        ]
        scores = jnp.where(block_mask[None], scores * score_scale, MASKED)
        row_max = jnp.max(scores, axis=-1, keepdims=True)
        weights = jnp.exp(scores - row_max)
        weights = (weights / jnp.sum(weights, axis=-1, keepdims=True)).astype(jnp.bfloat16)
        mixed_values = jnp.einsum(
            "hqk,khd->qhd", weights, kv_part[:, :, NOPE:], preferred_element_type=jnp.float32
        )
        outputs.append(mixed_values.reshape(query_span, OUT_WIDTH).astype(jnp.bfloat16))
    attn_out = jnp.concatenate(outputs, axis=0)
    inverse_count = 1.0 / all_tokens
    hessian = lax.psum_scatter(
        lax.dot_general(
            attn_out, attn_out, (((0,), (0,)), ((), ())), preferred_element_type=jnp.float32
        )
        * inverse_count,
        "dp",
        scatter_dimension=0,
        tiled=True,
    )
    return (attn_out, hessian)


def solution(mesh):
    placed = (P(("rep", "dp"), None), P(("rep", "dp"), None), P(), P("rep"))
    return jax.shard_map(
        per_device,
        mesh=mesh,
        in_specs=placed,
        out_specs=(P(("rep", "dp"), None), P(("rep", "dp"), None)),
        check_vma=False,
    )
```

profile of v0, /device:TPU:1, one launch (start us, length us, event | category | flops | bytes accessed | tf_op | source)
XLA Modules:
  0.0 310.1 jit_solution(5206243322617896533)
XLA Ops:
  8.1 4.5 %collective-permute-start = (bf16[128,576]{0,1:T(8,128)(2,1)S(1)}, bf16[128,576]{0,1:T(8,128)(2,1)S(1)}, u32[]{:S(2)}, u32[]{:S(2)}) collective-permute-start(bf16[128,576]{0,1:T(8,128)(2,1)S(1)} %slice.84), channel_id=1, source_target_pairs={{0,1},{1,2},{2,3},{3,4},{4,5},{5,6},{6,7},{7,8},{8,9},{9,10},{10,1... | collective-permute-start | bytes 442376 | tf_op jit(solution)/shard_map/ppermute | solution.py:24
  13.8 24.1 %while.49 = (s32[]{:T(128)}, u32[512]{0:T(512)S(1)}, u32[512]{0:T(512)S(1)}, s32[96]{0:T(128)S(1)}, s32[]{:T(128)}, /*index=5*/s32[]{:T(128)}, s32[]{:T(128)}, s32[]{}) while((s32[]{:T(128)}, u32[512]{0:T(512)S(1)}, u32[512]{0:T(512)S(1)}, s32[96]{0:T(128)S(1)}, s32[]{:T(128)}, /*index=5*/s32[]{:T(128)}, s32[]{:T(128)}, s32[]{}) %tuple.78), condition=%wide.region_4.5_spmd.clone, body=%wide.region_3.4_spmd.clone.sunk | while | flops 10756 | bytes 38001 | solution.py:47
  13.8 3.3 %gather_fusion.1 = s32[512]{0:T(512)S(1)} fusion(s32[96]{0:T(128)S(1)} %get-tuple-element.330, u32[1024]{0:T(1024)S(1)} %pad_clamp_fusion.5), kind=kCustom, calls=%fused_computation.1.clone.clone.1 | custom fusion | bytes 6144 | tf_op jit(solution)/shard_map/jit(searchsorted)/jit(_searchsorted_scan_impl)/vmap(jit(_searchsorted_scan_impl))/while/body/eval_jaxpr/gather | solution.py:47
  17.3 3.3 %gather_fusion.1 = s32[512]{0:T(512)S(1)} fusion(s32[96]{0:T(128)S(1)} %get-tuple-element.330, u32[1024]{0:T(1024)S(1)} %pad_clamp_fusion.5), kind=kCustom, calls=%fused_computation.1.clone.clone.1 | custom fusion | bytes 6144 | tf_op jit(solution)/shard_map/jit(searchsorted)/jit(_searchsorted_scan_impl)/vmap(jit(_searchsorted_scan_impl))/while/body/eval_jaxpr/gather | solution.py:47
  20.7 3.3 %gather_fusion.1 = s32[512]{0:T(512)S(1)} fusion(s32[96]{0:T(128)S(1)} %get-tuple-element.330, u32[1024]{0:T(1024)S(1)} %pad_clamp_fusion.5), kind=kCustom, calls=%fused_computation.1.clone.clone.1 | custom fusion | bytes 6144 | tf_op jit(solution)/shard_map/jit(searchsorted)/jit(_searchsorted_scan_impl)/vmap(jit(_searchsorted_scan_impl))/while/body/eval_jaxpr/gather | solution.py:47
  24.1 3.3 %gather_fusion.1 = s32[512]{0:T(512)S(1)} fusion(s32[96]{0:T(128)S(1)} %get-tuple-element.330, u32[1024]{0:T(1024)S(1)} %pad_clamp_fusion.5), kind=kCustom, calls=%fused_computation.1.clone.clone.1 | custom fusion | bytes 6144 | tf_op jit(solution)/shard_map/jit(searchsorted)/jit(_searchsorted_scan_impl)/vmap(jit(_searchsorted_scan_impl))/while/body/eval_jaxpr/gather | solution.py:47
  27.6 3.3 %gather_fusion.1 = s32[512]{0:T(512)S(1)} fusion(s32[96]{0:T(128)S(1)} %get-tuple-element.330, u32[1024]{0:T(1024)S(1)} %pad_clamp_fusion.5), kind=kCustom, calls=%fused_computation.1.clone.clone.1 | custom fusion | bytes 6144 | tf_op jit(solution)/shard_map/jit(searchsorted)/jit(_searchsorted_scan_impl)/vmap(jit(_searchsorted_scan_impl))/while/body/eval_jaxpr/gather | solution.py:47
  31.0 3.3 %gather_fusion.1 = s32[512]{0:T(512)S(1)} fusion(s32[96]{0:T(128)S(1)} %get-tuple-element.330, u32[1024]{0:T(1024)S(1)} %pad_clamp_fusion.5), kind=kCustom, calls=%fused_computation.1.clone.clone.1 | custom fusion | bytes 6144 | tf_op jit(solution)/shard_map/jit(searchsorted)/jit(_searchsorted_scan_impl)/vmap(jit(_searchsorted_scan_impl))/while/body/eval_jaxpr/gather | solution.py:47
  34.5 3.3 %gather_fusion.1 = s32[512]{0:T(512)S(1)} fusion(s32[96]{0:T(128)S(1)} %get-tuple-element.330, u32[1024]{0:T(1024)S(1)} %pad_clamp_fusion.5), kind=kCustom, calls=%fused_computation.1.clone.clone.1 | custom fusion | bytes 6144 | tf_op jit(solution)/shard_map/jit(searchsorted)/jit(_searchsorted_scan_impl)/vmap(jit(_searchsorted_scan_impl))/while/body/eval_jaxpr/gather | solution.py:47
  37.9 19.5 %while.48 = (s32[]{:T(128)}, u32[384]{0:T(512)S(1)}, u32[384]{0:T(512)S(1)}, s32[96]{0:T(128)S(1)}, s32[]{:T(128)}, /*index=5*/s32[]{:T(128)}, s32[]{:T(128)}, s32[]{}) while((s32[]{:T(128)}, u32[384]{0:T(512)S(1)}, u32[384]{0:T(512)S(1)}, s32[96]{0:T(128)S(1)}, s32[]{:T(128)}, /*index=5*/s32[]{:T(128)}, s32[]{:T(128)}, s32[]{}) %tuple.83), condition=%wide.region_2.3_spmd.clone, body=%wide.region_1.2_spmd.clone.sunk | while | flops 8324 | bytes 29553 | solution.py:46
  37.9 2.7 gather_fusion
  40.7 2.7 gather_fusion
  43.5 2.7 gather_fusion
  46.3 2.7 gather_fusion
  49.1 2.7 gather_fusion
  51.9 2.7 gather_fusion
  58.3 3.9 %fusion.51 = (bf16[128,6144]{1,0:T(8,128)(2,1)}, bf16[128,6144]{1,0:T(8,128)(2,1)S(1)}, bf16[128,6144]{1,0:T(8,128)(2,1)S(1)}) fusion(bf16[384,6144]{1,0:T(8,128)(2,1)} %param.8), kind=kLoop, calls=%fused_computation.79 | loop fusion | bytes 9437184 | tf_op jit(solution)/shard_map/slice | solution.py:67
  69.9 6.5 %convolution_convert_fusion = bf16[512,6144]{1,0:T(8,128)(2,1)S(1)} fusion(bf16[512,6144]{1,0:T(8,128)(2,1)} %param.10, bf16[512,576]{0,1:T(8,128)(2,1)S(1)} %constant_dynamic-update-slice_fusion), kind=kOutput, calls=%fused_computation.17 | convolution fusion | flops 3224371200 | bytes 13107200 | tf_op jit(solution)/shard_map/dot_general | solution.py:37
  76.4 3.0 fusion.50
  79.4 4.7 %copy.22 = bf16[256,6144]{0,1:T(8,128)(2,1)} copy(bf16[256,6144]{1,0:T(8,128)(2,1)} %get-tuple-element.200) | data formatting | bytes 6291456 | tf_op jit(solution)/shard_map/slice | solution.py:58
  93.3 4.7 %copy.26 = bf16[256,6144]{0,1:T(8,128)(2,1)} copy(bf16[256,6144]{1,0:T(8,128)(2,1)} %get-tuple-element.202) | data formatting | bytes 6291456 | tf_op jit(solution)/shard_map/slice | solution.py:58
  107.0 2.8 copy.29
  116.6 8.1 %convolution_multiply_fusion = f32[2048,2048]{1,0:T(8,128)} fusion(bf16[384,2048]{1,0:T(8,128)(2,1)S(1)} %pad_maximum_fusion), kind=kOutput, calls=%fused_computation.18 | convolution fusion | flops 3225419776 | bytes 18350080 | tf_op jit(solution)/shard_map/dot_general | solution.py:85
  124.7 178.5 %reduce-scatter.2.cloned.1.call-done = f32[128,2048]{1,0:T(8,128)} async-done(((f32[2048,2048]{1,0:T(8,128)}), f32[128,2048]{1,0:T(8,128)}) %reduce-scatter.2.cloned.1.call-update) | async-done | bytes 1048592 | tf_op jit(solution)/shard_map/reduce_scatter | solution.py:84
  (131 shorter events, 38.7 us)
Async XLA Ops:
  7.2 296.1 %reduce-scatter.2.cloned.1.call-start = ((), (), s32[]{:S(2)}) async-start(), calls=%async_computation.1 | async-start | bytes 17825792 | tf_op jit(solution)/shard_map/reduce_scatter | solution.py:84
  8.1 60.7 %collective-permute-start = (bf16[128,576]{0,1:T(8,128)(2,1)S(1)}, bf16[128,576]{0,1:T(8,128)(2,1)S(1)}, u32[]{:S(2)}, u32[]{:S(2)}) collective-permute-start(bf16[128,576]{0,1:T(8,128)(2,1)S(1)} %slice.84), channel_id=1, source_target_pairs={{0,1},{1,2},{2,3},{3,4},{4,5},{5,6},{6,7},{7,8},{8,9},{9,10},{10,1... | collective-permute-start | bytes 442376 | tf_op jit(solution)/shard_map/ppermute | solution.py:24
  84.2 2.0 copy-start.3
  86.2 1.3 copy-start.7
  98.0 2.0 copy-start.2
  100.0 1.3 copy-start.6
  109.8 2.0 copy-start.1
  114.4 2.0 copy-start.4
  114.4 2.0 copy-start.5
  116.6 8.1 %copy-start = (bf16[384,2048]{1,0:T(8,128)(2,1)}, bf16[384,2048]{1,0:T(8,128)(2,1)S(1)}, u32[]{:S(2)}) copy-start(bf16[384,2048]{1,0:T(8,128)(2,1)S(1)} %pad_maximum_fusion) | copy-start | bytes 4718596
Sparse Core Ops, SparseCore 0:
  124.9 178.3 reduce-scatter.1
where the time goes:
time: 311 us; the launch traced here: 310 us
  waiting for transfers between devices  179 us (58%)
  local copies, waits for them, and re-layouts  81.8 us (26%)
  matrix products  25.3 us (8%)
  between operations  14.3 us (5%)
  other arithmetic  4.77 us (2%)
  starting transfers between devices  4.58 us (1%)
    reduce_scatter x1, waiting for transfers between devices, per_device(): lax.psum_scatter(lax.dot_general(attn_out, attn_out, (((0,), (0,)), ((),...  178 us
    gather x7, local copies, waits for them, and re-layouts, per_device(): key_trace = jnp.searchsorted(trace_ends, key_pos, side='right')  23.4 us
    gather x7, local copies, waits for them, and re-layouts, per_device(): query_trace = jnp.searchsorted(trace_ends, query_pos, side='right')  18.8 us
    slice x4, local copies, waits for them, and re-layouts, per_device(): kv_part = window_kv[block_first:block_first + key_span]  15.3 us
    slice x4, local copies, waits for them, and re-layouts, per_device(): query_part = query_heads[block_first:block_first + query_span]  9.62 us
    dot_general x1, matrix products, per_device(): lax.dot_general(attn_out, attn_out, (((0,), (0,)), ((), ())), preferred_e...  8.1 us
    dot_general x3, matrix products, per_device(): jnp.einsum('hqk,khd->qhd', weights, kv_part[:, :, NOPE:], preferred_eleme...  6.79 us
    dot_general x1, matrix products, per_device(): jnp.dot(window_latent[:, :KV_RANK], kv_weight, preferred_element_type=jnp...  6.48 us
  transfers between devices with their start and end apart: 2, of which 1 were waited for; matrix products, arithmetic and copies ran while one was open for 18% of the time, Pallas kernels for 0%

commit v1 on v0

v1 whole, which is shorter than its diff:
```python
import math

import jax
import jax.numpy as jnp
from jax import lax
from jax.experimental import pallas as pl
from jax.experimental.pallas import tpu as pltpu
from jax.sharding import PartitionSpec as P

HEADS = 32
NOPE = 128
ROPE = 64
V_DIM = 64
KV_RANK = 512
MAXLEN = 128
OUT_WIDTH = 2048

MASKED = -1e30
BLOCK = 128
HEAD_WIDTH = NOPE + ROPE
PAIR = 2 * HEAD_WIDTH
PAIRS_PER_STEP = 2
STRIP = 9 * BLOCK
MESH = pl.DeviceIdType.MESH
EXP_SCALE = math.log2(math.e) / math.sqrt(NOPE + ROPE)


def attention_kernel(window_ref, start_ref, weight_ref, query_ref, out_ref, bias_ref):
    rows = query_ref.shape[0]
    blocks = rows // BLOCK

    @pl.when(pl.program_id(0) == 0)
    def _():
        for b in range(blocks):
            start = start_ref[b * BLOCK : (b + 1) * BLOCK, :]
            key = lax.broadcasted_iota(jnp.int32, (BLOCK, 2 * BLOCK), 1) + (b - 1) * BLOCK
            query = lax.broadcasted_iota(jnp.int32, (BLOCK, 2 * BLOCK), 0) + b * BLOCK
            allowed = (key <= query) & (key >= start)
            bias_ref[b * BLOCK : (b + 1) * BLOCK, :] = jnp.where(allowed, 0.0, MASKED)

    content = window_ref[:, :KV_RANK]
    rope_low = window_ref[:, KV_RANK : KV_RANK + 128]
    rope_high = window_ref[:, KV_RANK + 128 :]
    keys_rows = window_ref.shape[0]
    low = lax.broadcasted_iota(jnp.int32, (keys_rows, 128), 1) < 64
    low_out = lax.broadcasted_iota(jnp.int32, (BLOCK, 128), 1) < 64
    one = jnp.ones((keys_rows, 128), jnp.bfloat16)
    zero = jnp.zeros((keys_rows, 128), jnp.bfloat16)
    for pair in range(PAIRS_PER_STEP):
        at = pair * PAIR
        kv = jnp.dot(
            content, weight_ref[:, at : at + PAIR], preferred_element_type=jnp.float32
        ).astype(jnp.bfloat16)
        first, second, third = kv[:, :128], kv[:, 128:256], kv[:, 256:384]
        keys = (
            jnp.concatenate([first, rope_low], axis=1),
            jnp.concatenate(
                [jnp.where(low, zero, second), jnp.where(low, third, rope_high)], axis=1
            ),
        )
        values = (jnp.where(low, second, one), jnp.where(low, one, third))
        for b in range(blocks):
            rows_at = slice(b * BLOCK, (b + 1) * BLOCK)
            keys_at = slice(b * BLOCK, (b + 2) * BLOCK)
            bias = bias_ref[rows_at, :]
            mixed = []
            for head in range(2):
                query = query_ref[rows_at, at + head * 128 : at + head * 128 + 256]
                scores = lax.dot_general(
                    query,
                    keys[head][keys_at],
                    (((1,), (1,)), ((), ())),
                    preferred_element_type=jnp.float32,
                )
                scores = scores + bias
                top = jnp.max(scores, axis=1, keepdims=True)
                weights = jnp.exp2((scores - top) * EXP_SCALE).astype(jnp.bfloat16)
                mixed.append(
                    jnp.dot(weights, values[head][keys_at], preferred_element_type=jnp.float32)
                )
            total = pltpu.roll(jnp.where(low_out, mixed[1], mixed[0]), 64, 1)
            result = jnp.where(low_out, mixed[0], mixed[1]) / total
            out_ref[rows_at, pair * 128 : (pair + 1) * 128] = result.astype(jnp.bfloat16)


def attention(window, start, kv_weight, queries):
    rows = queries.shape[0]
    span = PAIR * PAIRS_PER_STEP
    return pl.pallas_call(
        attention_kernel,
        grid=(queries.shape[1] // span,),
        in_specs=[
            pl.BlockSpec(window.shape, lambda i: (0, 0)),
            pl.BlockSpec(start.shape, lambda i: (0, 0)),
            pl.BlockSpec((KV_RANK, span), lambda i: (0, i)),
            pl.BlockSpec((rows, span), lambda i: (0, i)),
        ],
        out_specs=pl.BlockSpec((rows, PAIRS_PER_STEP * 128), lambda i: (0, i)),
        out_shape=jax.ShapeDtypeStruct((rows, OUT_WIDTH), jnp.bfloat16),
        scratch_shapes=[pltpu.VMEM((rows, 2 * BLOCK), jnp.float32)],
        compiler_params=pltpu.CompilerParams(vmem_limit_bytes=40 * 1024 * 1024),
    )(window, start, kv_weight, queries)


def hessian_kernel(
    devices,
    inverse_count,
    a_ref,
    out_ref,
    a_all,
    y_send,
    y_recv,
    z_send,
    z_recv,
    t_send,
    t_recv,
    local_sem,
    pair_send_sem,
    pair_recv_sem,
    y_send_sem,
    y_recv_sem,
    z_send_sem,
    z_recv_sem,
    t_send_sem,
    t_recv_sem,
):
    rows = a_ref.shape[0]
    extra = STRIP - BLOCK
    zs = devices // 4
    me = lax.axis_index("dp")
    rep = lax.axis_index("rep")
    core = lax.rem(me, 2)
    y = lax.rem(me // 2, 2)
    z = me // 4

    def index_of(z_at, y_at):
        return (z_at * 2 + y_at) * 2 + core

    def other(k):
        return lax.rem(me + k, devices)

    partner = z * 4 + y * 2 + (1 - core)

    barrier = pltpu.get_barrier_semaphore()
    for k in range(1, devices):
        pl.semaphore_signal(barrier, inc=1, device_id=(rep, other(k)), device_id_type=MESH)
    own = [
        pltpu.make_async_copy(a_ref, a_all.at[0:rows, 0:OUT_WIDTH], local_sem.at[0]),
        pltpu.make_async_copy(
            a_ref.at[:, 0:extra],
            a_all.at[0:rows, OUT_WIDTH : OUT_WIDTH + extra],
            local_sem.at[1],
        ),
    ]
    for copy in own:
        copy.start()
    pl.semaphore_wait(barrier, devices - 1)

    pair_copies = [
        pltpu.make_async_remote_copy(
            src_ref=a_ref,
            dst_ref=a_all.at[rows : 2 * rows, 0:OUT_WIDTH],
            send_sem=pair_send_sem.at[0],
            recv_sem=pair_recv_sem.at[0],
            device_id=(rep, partner),
            device_id_type=MESH,
        ),
        pltpu.make_async_remote_copy(
            src_ref=a_ref.at[:, 0:extra],
            dst_ref=a_all.at[rows : 2 * rows, OUT_WIDTH : OUT_WIDTH + extra],
            send_sem=pair_send_sem.at[1],
            recv_sem=pair_recv_sem.at[1],
            device_id=(rep, partner),
            device_id_type=MESH,
        ),
    ]
    for copy in pair_copies:
        copy.start()
    for copy in own:
        copy.wait()
    for copy in pair_copies:
        copy.wait()

    def strip(owner):
        at = pl.multiple_of(owner * BLOCK, BLOCK)
        return lax.dot_general(
            a_all[:, pl.ds(at, BLOCK)],
            a_all[:, pl.ds(at, STRIP)],
            (((0,), (0,)), ((), ())),
            preferred_element_type=jnp.float32,
        )

    y_copies = []
    for j in range(zs):
        z_at = lax.rem(z + 1 + j, zs)
        y_send[j] = strip(index_of(z_at, 1 - y)).astype(jnp.bfloat16)
        copy = pltpu.make_async_remote_copy(
            src_ref=y_send.at[j],
            dst_ref=y_recv.at[j],
            send_sem=y_send_sem.at[j],
            recv_sem=y_recv_sem.at[j],
            device_id=(rep, index_of(z, 1 - y)),
            device_id_type=MESH,
        )
        copy.start()
        y_copies.append(copy)

    z_copies = []
    for j in range(zs):
        z_at = lax.rem(z + 1 + j, zs)
        mine = strip(index_of(z_at, y))
        y_copies[j].wait_recv()
        mine = mine + y_recv[j].astype(jnp.float32)
        if j < zs - 1:
            z_send[j] = mine.astype(jnp.bfloat16)
            copy = pltpu.make_async_remote_copy(
                src_ref=z_send.at[j],
                dst_ref=z_recv.at[j],
                send_sem=z_send_sem.at[j],
                recv_sem=z_recv_sem.at[j],
                device_id=(rep, index_of(z_at, y)),
                device_id_type=MESH,
            )
            copy.start()
            z_copies.append(copy)
        else:
            total = mine
    for j in range(zs - 1):
        z_copies[j].wait_recv()
        total = total + z_recv[j].astype(jnp.float32)
    total = total * inverse_count

    t_copies = []
    for k in range(1, 8):
        t_send[k - 1] = total[:, k * BLOCK : (k + 1) * BLOCK].T.astype(jnp.bfloat16)
        copy = pltpu.make_async_remote_copy(
            src_ref=t_send.at[k - 1],
            dst_ref=t_recv.at[k - 1],
            send_sem=t_send_sem.at[k - 1],
            recv_sem=t_recv_sem.at[k - 1],
            device_id=(rep, other(k)),
            device_id_type=MESH,
        )
        copy.start()
        t_copies.append(copy)
    for k in range(9):
        at = pl.multiple_of(other(k) * BLOCK, BLOCK)
        out_ref[:, pl.ds(at, BLOCK)] = total[:, k * BLOCK : (k + 1) * BLOCK]
    for k in range(1, 8):
        t_copies[k - 1].wait_recv()
        at = pl.multiple_of(other(devices - k) * BLOCK, BLOCK)
        out_ref[:, pl.ds(at, BLOCK)] = t_recv[k - 1].astype(jnp.float32)
    for copy in y_copies + z_copies + t_copies:
        copy.wait_send()


def fused_hessian(attn_out, devices, inverse_count):
    rows = attn_out.shape[0]
    zs = devices // 4
    vmem = pl.BlockSpec(memory_space=pltpu.VMEM)

    def body(*refs):
        hessian_kernel(devices, inverse_count, *refs)

    return pl.pallas_call(
        body,
        out_shape=jax.ShapeDtypeStruct((BLOCK, OUT_WIDTH), jnp.float32),
        in_specs=[vmem],
        out_specs=vmem,
        scratch_shapes=[
            pltpu.VMEM((2 * rows, OUT_WIDTH + STRIP - BLOCK), jnp.bfloat16),
            pltpu.VMEM((zs, BLOCK, STRIP), jnp.bfloat16),
            pltpu.VMEM((zs, BLOCK, STRIP), jnp.bfloat16),
            pltpu.VMEM((zs - 1, BLOCK, STRIP), jnp.bfloat16),
            pltpu.VMEM((zs - 1, BLOCK, STRIP), jnp.bfloat16),
            pltpu.VMEM((7, BLOCK, BLOCK), jnp.bfloat16),
            pltpu.VMEM((7, BLOCK, BLOCK), jnp.bfloat16),
            pltpu.SemaphoreType.DMA((2,)),
            pltpu.SemaphoreType.DMA((2,)),
            pltpu.SemaphoreType.DMA((2,)),
            pltpu.SemaphoreType.DMA((zs,)),
            pltpu.SemaphoreType.DMA((zs,)),
            pltpu.SemaphoreType.DMA((zs - 1,)),
            pltpu.SemaphoreType.DMA((zs - 1,)),
            pltpu.SemaphoreType.DMA((7,)),
            pltpu.SemaphoreType.DMA((7,)),
        ],
        compiler_params=pltpu.CompilerParams(
            collective_id=0, has_side_effects=True, vmem_limit_bytes=40 * 1024 * 1024
        ),
    )(attn_out)


def per_device(queries, latents, kv_weight, lengths):
    devices = lax.axis_size("dp")
    device = lax.axis_index("dp")
    rows = queries.shape[0]
    inverse_count = 1.0 / (rows * devices)
    halo = lax.ppermute(
        latents[rows - MAXLEN :], "dp", [(source, source + 1) for source in range(devices - 1)]
    )
    window = jnp.concatenate([halo, latents], axis=0)
    rope = window[:, KV_RANK:]
    blank = jnp.zeros((rows + MAXLEN, 2 * (128 - ROPE)), window.dtype)
    window = jnp.concatenate([window, blank, rope], axis=1)

    traces = lengths.shape[0]
    order = jnp.arange(traces, dtype=jnp.int32)
    ends = jnp.sum(jnp.where(order[None, :] <= order[:, None], lengths[None, :], 0), axis=1)
    first_row = device * rows
    position = first_row + jnp.arange(rows, dtype=jnp.int32)
    start = jnp.max(jnp.where(ends[None, :] <= position[:, None], ends[None, :], 0), axis=1)
    start = (start - first_row)[:, None]

    attn_out = attention(window, start, kv_weight, queries)
    if devices * BLOCK == OUT_WIDTH:
        return attn_out, fused_hessian(attn_out, devices, inverse_count)
    partial = lax.dot_general(
        attn_out, attn_out, (((0,), (0,)), ((), ())), preferred_element_type=jnp.float32
    )
    hessian = lax.psum_scatter(partial, "dp", scatter_dimension=0, tiled=True)
    return attn_out, hessian * inverse_count


def solution(mesh):
    placed = (P(("rep", "dp"), None), P(("rep", "dp"), None), P(), P("rep"))
    return jax.shard_map(
        per_device,
        mesh=mesh,
        in_specs=placed,
        out_specs=(P(("rep", "dp"), None), P(("rep", "dp"), None)),
        check_vma=False,
    )
```

time: 311 us -> 99.9 us (0.32)
  waiting for transfers between devices: 179 us -> 1.14 us
  Pallas kernels: 0 us -> 83.1 us
  local copies, waits for them, and re-layouts: 81.8 us -> 8.96 us
  matrix products: 25.3 us -> 0 us
  between operations: 14.3 us -> 0.71 us
  other arithmetic: 4.77 us -> 1.07 us
    reduce_scatter x1 -> x0, waiting for transfers between devices: 178 us -> none  [per_device(): lax.psum_scatter(lax.dot_general(attn_out, attn_out, (((0,), (0,)), ((),...]
    pallas_call x0 -> x2, Pallas kernels: none -> 83.1 us  [the longest x1 51.9 us: fused_hessian(): pl.pallas_call(body, out_shape=jax.ShapeDtypeStruct((BLOCK, OUT_WIDTH), j...]
    gather x14 -> x0, local copies, waits for them, and re-layouts: 42.3 us -> none  [the longest x7 23.4 us: per_device(): key_trace = jnp.searchsorted(trace_ends, key_pos, side='right')]
    slice x15 -> x1, local copies, waits for them, and re-layouts: 32.8 us -> 0.02 us  [per_device(): latents[rows - MAXLEN:]]
    dot_general x8 -> x0, matrix products: 25.3 us -> none  [the longest x1 8.1 us: per_device(): lax.dot_general(attn_out, attn_out, (((0,), (0,)), ((), ())), preferred_e...]
    unnamed x17 -> x8, local copies, waits for them, and re-layouts: 0.25 us -> 8.76 us
    convert_element_type x3 -> x0, local copies, waits for them, and re-layouts: 4.31 us -> none  [per_device(): mixed_values.reshape(query_span, OUT_WIDTH).astype(jnp.bfloat16)]
    sub x3 -> x1, other arithmetic: 3.52 us -> 0.01 us  [per_device(): start = (start - first_row)[:, None]]
  transfers between devices with their start and end apart: 2 -> 1, of which waited for: 1 -> 1; matrix products, arithmetic and copies ran while one was open for 18% -> 1% of each run, Pallas kernels for 0% -> 0%
where the time goes in v1:
time: 99.9 us; the launch traced here: 99.5 us
  Pallas kernels  83.1 us (83%)
  local copies, waits for them, and re-layouts  8.96 us (9%)
  starting transfers between devices  4.54 us (5%)
  waiting for transfers between devices  1.14 us (1%)
  other arithmetic  1.07 us (1%)
    pallas_call x1, Pallas kernels, fused_hessian(): pl.pallas_call(body, out_shape=jax.ShapeDtypeStruct((BLOCK, OUT_WIDTH), j...  51.9 us
    pallas_call x1, Pallas kernels, attention(): pl.pallas_call(attention_kernel, grid=(queries.shape[1] // span,), in_spe...  31.2 us
    unnamed x8, local copies, waits for them, and re-layouts  8.76 us
    ppermute x1, starting transfers between devices, per_device(): lax.ppermute(latents[rows - MAXLEN:], 'dp', [(source, source + 1) for sou...  4.54 us
  transfers between devices with their start and end apart: 1, of which 1 were waited for; matrix products, arithmetic and copies ran while one was open for 1% of the time, Pallas kernels for 0%

profile of v1, /device:TPU:1, one launch (start us, length us, event | category | flops | bytes accessed | tf_op | source)
XLA Modules:
  0.0 99.5 jit_solution(10842854173041024166)
XLA Ops:
  0.6 1.3 %copy.11 = bf16[384,576]{1,0:T(8,128)(2,1)S(1)} copy(bf16[384,576]{0,1:T(8,128)(2,1)} %param.5) | data formatting | bytes 884736 | tf_op args[1]
  1.9 4.5 %collective-permute-start = (bf16[128,576]{1,0:T(8,128)(2,1)S(1)}, bf16[128,576]{1,0:T(8,128)(2,1)S(1)}, u32[]{:S(2)}, u32[]{:S(2)}) collective-permute-start(bf16[128,576]{1,0:T(8,128)(2,1)S(1)} %slice.8), channel_id=1, source_target_pairs={{0,1},{1,2},{2,3},{3,4},{4,5},{5,6},{6,7},{7,8},{8,9},{9,10},{10,1... | collective-permute-start | bytes 442376 | tf_op jit(solution)/shard_map/ppermute | solution.py:299
  6.5 0.8 select_reduce_fusion.1
  7.2 0.1 select_reduce_fusion
  7.4 0.1 sub.16.start_ref
  7.5 0.1 pad.2.clone
  7.6 1.1 %collective-permute-done = bf16[128,576]{1,0:T(8,128)(2,1)S(1)} collective-permute-done((bf16[128,576]{1,0:T(8,128)(2,1)S(1)}, bf16[128,576]{1,0:T(8,128)(2,1)S(1)}, u32[]{:S(2)}, u32[]{:S(2)}) %collective-permute-start) | collective-permute-done | bytes 147488 | tf_op jit(solution)/shard_map/ppermute | solution.py:299
  8.7 0.2 fusion.3.window_ref
  8.9 0.0 copy-start
  8.9 2.8 %copy-done = bf16[512,6144]{1,0:T(8,128)(2,1)S(1)} copy-done((bf16[512,6144]{1,0:T(8,128)(2,1)S(1)}, bf16[512,6144]{1,0:T(8,128)(2,1)}, u32[]{:S(2)}) %copy-start) | copy-done | bytes 6291480
  11.7 0.0 copy-start.2
  11.7 2.3 %copy-done.2 = bf16[384,6144]{1,0:T(8,128)(2,1)S(1)} copy-done((bf16[384,6144]{1,0:T(8,128)(2,1)S(1)}, bf16[384,6144]{1,0:T(8,128)(2,1)}, u32[]{:S(2)}) %copy-start.2) | copy-done | bytes 4718616
  14.0 31.2 %shard_map.59.refs_0_ = bf16[384,2048]{1,0:T(8,128)(2,1)} custom-call(bf16[512,768]{1,0:T(8,128)(2,1)S(1)} %fusion.3.window_ref, s32[384,1]{1,0:T(8,128)S(1)} %sub.16.start_ref, bf16[512,6144]{1,0:T(8,128)(2,1)S(1)} %copy-done, bf16[384,6144]{1,0:T(8,128)(2,1)S(1)} %copy-done.2), custom_call_target="tpu_custom_call" | custom-call | tf_op jit(solution)/shard_map/pallas_call | solution.py:89
  45.3 0.0 copy-start.1
  45.3 1.4 %copy-done.1 = bf16[384,2048]{1,0:T(8,128)(2,1)S(1)} copy-done((bf16[384,2048]{1,0:T(8,128)(2,1)S(1)}, bf16[384,2048]{1,0:T(8,128)(2,1)}, u32[]{:S(2)}) %copy-start.1) | copy-done | bytes 1572888
  46.7 51.9 %shard_map.60 = f32[128,2048]{1,0:T(8,128)S(1)} custom-call(bf16[384,2048]{1,0:T(8,128)(2,1)S(1)} %copy-done.1), custom_call_target="tpu_custom_call" | custom-call | tf_op jit(solution)/shard_map/pallas_call | solution.py:265
  98.5 1.0 copy.15
  (4 shorter events, 0.0 us)
Async XLA Ops:
  1.9 6.8 %collective-permute-start = (bf16[128,576]{1,0:T(8,128)(2,1)S(1)}, bf16[128,576]{1,0:T(8,128)(2,1)S(1)}, u32[]{:S(2)}, u32[]{:S(2)}) collective-permute-start(bf16[128,576]{1,0:T(8,128)(2,1)S(1)} %slice.8), channel_id=1, source_target_pairs={{0,1},{1,2},{2,3},{3,4},{4,5},{5,6},{6,7},{7,8},{8,9},{9,10},{10,1... | collective-permute-start | bytes 442376 | tf_op jit(solution)/shard_map/ppermute | solution.py:299
  8.9 2.8 %copy-start = (bf16[512,6144]{1,0:T(8,128)(2,1)S(1)}, bf16[512,6144]{1,0:T(8,128)(2,1)}, u32[]{:S(2)}) copy-start(bf16[512,6144]{1,0:T(8,128)(2,1)} %weight_ref.1) | copy-start | bytes 18874372
  11.7 2.3 %copy-start.2 = (bf16[384,6144]{1,0:T(8,128)(2,1)S(1)}, bf16[384,6144]{1,0:T(8,128)(2,1)}, u32[]{:S(2)}) copy-start(bf16[384,6144]{1,0:T(8,128)(2,1)} %query_ref.1) | copy-start | bytes 14155780
  45.3 1.4 %copy-start.1 = (bf16[384,2048]{1,0:T(8,128)(2,1)S(1)}, bf16[384,2048]{1,0:T(8,128)(2,1)}, u32[]{:S(2)}) copy-start(bf16[384,2048]{1,0:T(8,128)(2,1)} %shard_map.59.refs_0_) | copy-start | bytes 4718596

commit v2 on v1

v2 whole, which is shorter than its diff:
```python
import math

import jax
import jax.numpy as jnp
from jax import lax
from jax.experimental import pallas as pl
from jax.experimental.pallas import tpu as pltpu
from jax.sharding import PartitionSpec as P

HEADS = 32
NOPE = 128
ROPE = 64
V_DIM = 64
KV_RANK = 512
MAXLEN = 128
OUT_WIDTH = 2048

MASKED = -1e30
BLOCK = 128
HEAD_WIDTH = NOPE + ROPE
PAIR = 2 * HEAD_WIDTH
PAIRS_PER_STEP = 2
STRIP = 9 * BLOCK
LAG = 2
MESH = pl.DeviceIdType.MESH
EXP_SCALE = math.log2(math.e) / math.sqrt(NOPE + ROPE)


def attention_kernel(window_ref, start_ref, weight_ref, query_ref, out_ref, bias_ref):
    rows = query_ref.shape[0]
    blocks = rows // BLOCK

    @pl.when(pl.program_id(0) == 0)
    def _():
        for b in range(blocks):
            start = start_ref[b * BLOCK : (b + 1) * BLOCK, :]
            key = lax.broadcasted_iota(jnp.int32, (BLOCK, 2 * BLOCK), 1) + (b - 1) * BLOCK
            query = lax.broadcasted_iota(jnp.int32, (BLOCK, 2 * BLOCK), 0) + b * BLOCK
            allowed = (key <= query) & (key >= start)
            bias_ref[b * BLOCK : (b + 1) * BLOCK, :] = jnp.where(allowed, 0.0, MASKED)

    content = window_ref[:, :KV_RANK]
    rope_low = window_ref[:, KV_RANK : KV_RANK + 128]
    rope_high = window_ref[:, KV_RANK + 128 :]
    keys_rows = window_ref.shape[0]
    low = lax.broadcasted_iota(jnp.int32, (keys_rows, 128), 1) < 64
    low_out = lax.broadcasted_iota(jnp.int32, (BLOCK, 128), 1) < 64
    one = jnp.ones((keys_rows, 128), jnp.bfloat16)
    zero = jnp.zeros((keys_rows, 128), jnp.bfloat16)
    for pair in range(PAIRS_PER_STEP):
        at = pair * PAIR
        kv = jnp.dot(
            content, weight_ref[:, at : at + PAIR], preferred_element_type=jnp.float32
        ).astype(jnp.bfloat16)
        first, second, third = kv[:, :128], kv[:, 128:256], kv[:, 256:384]
        keys = (
            jnp.concatenate([first, rope_low], axis=1),
            jnp.concatenate(
                [jnp.where(low, zero, second), jnp.where(low, third, rope_high)], axis=1
            ),
        )
        values = (jnp.where(low, second, one), jnp.where(low, one, third))
        for b in range(blocks):
            rows_at = slice(b * BLOCK, (b + 1) * BLOCK)
            keys_at = slice(b * BLOCK, (b + 2) * BLOCK)
            bias = bias_ref[rows_at, :]
            mixed = []
            for head in range(2):
                query = query_ref[rows_at, at + head * 128 : at + head * 128 + 256]
                scores = lax.dot_general(
                    query,
                    keys[head][keys_at],
                    (((1,), (1,)), ((), ())),
                    preferred_element_type=jnp.float32,
                )
                scores = scores + bias
                top = jnp.max(scores, axis=1, keepdims=True)
                weights = jnp.exp2((scores - top) * EXP_SCALE).astype(jnp.bfloat16)
                mixed.append(
                    jnp.dot(weights, values[head][keys_at], preferred_element_type=jnp.float32)
                )
            total = pltpu.roll(jnp.where(low_out, mixed[1], mixed[0]), 64, 1)
            result = jnp.where(low_out, mixed[0], mixed[1]) / total
            out_ref[rows_at, pair * 128 : (pair + 1) * 128] = result.astype(jnp.bfloat16)


def attention(window, start, kv_weight, queries):
    rows = queries.shape[0]
    span = PAIR * PAIRS_PER_STEP
    return pl.pallas_call(
        attention_kernel,
        grid=(queries.shape[1] // span,),
        in_specs=[
            pl.BlockSpec(window.shape, lambda i: (0, 0)),
            pl.BlockSpec(start.shape, lambda i: (0, 0)),
            pl.BlockSpec((KV_RANK, span), lambda i: (0, i)),
            pl.BlockSpec((rows, span), lambda i: (0, i)),
        ],
        out_specs=pl.BlockSpec((rows, PAIRS_PER_STEP * 128), lambda i: (0, i)),
        out_shape=jax.ShapeDtypeStruct((rows, OUT_WIDTH), jnp.bfloat16),
        scratch_shapes=[pltpu.VMEM((rows, 2 * BLOCK), jnp.float32)],
        compiler_params=pltpu.CompilerParams(vmem_limit_bytes=40 * 1024 * 1024),
    )(window, start, kv_weight, queries)


def fused_kernel(
    devices,
    inverse_count,
    window_ref,
    start_ref,
    weight_ref,
    query_ref,
    out_ref,
    hessian_ref,
    bias_ref,
    a_all,
    z_send,
    z_recv,
    t_send,
    t_recv,
    pair_send_sem,
    pair_recv_sem,
    y_send_sem,
    y_recv_sem,
    pass_send_sem,
    pass_recv_sem,
    z_send_sem,
    z_recv_sem,
    t_send_sem,
    t_recv_sem,
):
    rows = query_ref.shape[0]
    width = out_ref.shape[1]
    steps = OUT_WIDTH // width
    zs = devices // 4
    step = pl.program_id(0)
    me = lax.axis_index("dp")
    rep = lax.axis_index("rep")
    core = lax.rem(me, 2)
    y = lax.rem(me // 2, 2)
    z = me // 4

    def index_of(z_at, y_at, core_at):
        return (z_at * 2 + y_at) * 2 + core_at

    def other(k):
        return lax.rem(me + k, devices)

    partner = index_of(z, y, 1 - core)
    across = index_of(z, 1 - y, core)

    def piece_copy(source, target, piece, send_sem, recv_sem, device):
        at = pl.ds(pl.multiple_of(piece * width, width), width)
        return pltpu.make_async_remote_copy(
            src_ref=a_all.at[source * rows : (source + 1) * rows, at],
            dst_ref=a_all.at[target * rows : (target + 1) * rows, at],
            send_sem=send_sem.at[piece],
            recv_sem=recv_sem.at[piece],
            device_id=(rep, device),
            device_id_type=MESH,
        )

    def pair_copy(piece):
        return piece_copy(0, 1, piece, pair_send_sem, pair_recv_sem, partner)

    def y_copy(piece):
        return piece_copy(0, 2, piece, y_send_sem, y_recv_sem, across)

    def pass_copy(piece):
        return piece_copy(2, 3, piece, pass_send_sem, pass_recv_sem, partner)

    @pl.when(step == 0)
    def _():
        barrier = pltpu.get_barrier_semaphore()
        for k in range(1, devices):
            pl.semaphore_signal(barrier, inc=1, device_id=(rep, other(k)), device_id_type=MESH)

    attention_kernel(window_ref, start_ref, weight_ref, query_ref, out_ref, bias_ref)
    a_all[0:rows, pl.ds(pl.multiple_of(step * width, width), width)] = out_ref[...]

    @pl.when(step == 0)
    def _():
        pl.semaphore_wait(pltpu.get_barrier_semaphore(), devices - 1)

    y_copy(step).start()
    pair_copy(step).start()

    @pl.when(step >= LAG)
    def _():
        y_copy(step - LAG).wait_recv()
        pass_copy(step - LAG).start()

    @pl.when(step == steps - 1)
    def _():
        for piece in range(steps - LAG, steps):
            y_copy(piece).wait_recv()
            pass_copy(piece).start()
        for piece in range(steps):
            pair_copy(piece).wait_recv()
            pass_copy(piece).wait_recv()
        a_all[:, OUT_WIDTH:] = a_all[:, : STRIP - BLOCK]

        def strip(owner):
            at = pl.multiple_of(owner * BLOCK, BLOCK)
            return lax.dot_general(
                a_all[:, pl.ds(at, BLOCK)],
                a_all[:, pl.ds(at, STRIP)],
                (((0,), (0,)), ((), ())),
                preferred_element_type=jnp.float32,
            )

        z_copies = []
        for j in range(zs - 1):
            target = index_of(lax.rem(z + 1 + j, zs), y, core)
            z_send[j] = strip(target).astype(jnp.bfloat16)
            copy = pltpu.make_async_remote_copy(
                src_ref=z_send.at[j],
                dst_ref=z_recv.at[j],
                send_sem=z_send_sem.at[j],
                recv_sem=z_recv_sem.at[j],
                device_id=(rep, target),
                device_id_type=MESH,
            )
            copy.start()
            z_copies.append(copy)
        total = strip(me)
        for j in range(zs - 1):
            z_copies[j].wait_recv()
            total = total + z_recv[j].astype(jnp.float32)
        total = total * inverse_count

        t_copies = []
        for k in range(1, 8):
            t_send[k - 1] = total[:, k * BLOCK : (k + 1) * BLOCK].T.astype(jnp.bfloat16)
            copy = pltpu.make_async_remote_copy(
                src_ref=t_send.at[k - 1],
                dst_ref=t_recv.at[k - 1],
                send_sem=t_send_sem.at[k - 1],
                recv_sem=t_recv_sem.at[k - 1],
                device_id=(rep, other(k)),
                device_id_type=MESH,
            )
            copy.start()
            t_copies.append(copy)
        for k in range(9):
            at = pl.multiple_of(other(k) * BLOCK, BLOCK)
            hessian_ref[:, pl.ds(at, BLOCK)] = total[:, k * BLOCK : (k + 1) * BLOCK]
        for k in range(1, 8):
            t_copies[k - 1].wait_recv()
            at = pl.multiple_of(other(devices - k) * BLOCK, BLOCK)
            hessian_ref[:, pl.ds(at, BLOCK)] = t_recv[k - 1].astype(jnp.float32)
        for piece in range(steps):
            pair_copy(piece).wait_send()
            y_copy(piece).wait_send()
            pass_copy(piece).wait_send()
        for copy in z_copies + t_copies:
            copy.wait_send()


def fused(window, start, kv_weight, queries, devices, inverse_count):
    rows = queries.shape[0]
    span = PAIR * PAIRS_PER_STEP
    steps = queries.shape[1] // span
    zs = devices // 4

    def body(*refs):
        fused_kernel(devices, inverse_count, *refs)

    return pl.pallas_call(
        body,
        grid=(steps,),
        in_specs=[
            pl.BlockSpec(window.shape, lambda i: (0, 0)),
            pl.BlockSpec(start.shape, lambda i: (0, 0)),
            pl.BlockSpec((KV_RANK, span), lambda i: (0, i)),
            pl.BlockSpec((rows, span), lambda i: (0, i)),
        ],
        out_specs=[
            pl.BlockSpec((rows, PAIRS_PER_STEP * 128), lambda i: (0, i)),
            pl.BlockSpec((BLOCK, OUT_WIDTH), lambda i: (0, 0)),
        ],
        out_shape=[
            jax.ShapeDtypeStruct((rows, OUT_WIDTH), jnp.bfloat16),
            jax.ShapeDtypeStruct((BLOCK, OUT_WIDTH), jnp.float32),
        ],
        scratch_shapes=[
            pltpu.VMEM((rows, 2 * BLOCK), jnp.float32),
            pltpu.VMEM((4 * rows, OUT_WIDTH + STRIP - BLOCK), jnp.bfloat16),
            pltpu.VMEM((zs - 1, BLOCK, STRIP), jnp.bfloat16),
            pltpu.VMEM((zs - 1, BLOCK, STRIP), jnp.bfloat16),
            pltpu.VMEM((7, BLOCK, BLOCK), jnp.bfloat16),
            pltpu.VMEM((7, BLOCK, BLOCK), jnp.bfloat16),
            pltpu.SemaphoreType.DMA((steps,)),
            pltpu.SemaphoreType.DMA((steps,)),
            pltpu.SemaphoreType.DMA((steps,)),
            pltpu.SemaphoreType.DMA((steps,)),
            pltpu.SemaphoreType.DMA((steps,)),
            pltpu.SemaphoreType.DMA((steps,)),
            pltpu.SemaphoreType.DMA((zs - 1,)),
            pltpu.SemaphoreType.DMA((zs - 1,)),
            pltpu.SemaphoreType.DMA((7,)),
            pltpu.SemaphoreType.DMA((7,)),
        ],
        compiler_params=pltpu.CompilerParams(
            collective_id=0, has_side_effects=True, vmem_limit_bytes=60 * 1024 * 1024
        ),
    )(window, start, kv_weight, queries)


def per_device(queries, latents, kv_weight, lengths):
    devices = lax.axis_size("dp")
    device = lax.axis_index("dp")
    rows = queries.shape[0]
    inverse_count = 1.0 / (rows * devices)
    halo = lax.ppermute(
        latents[rows - MAXLEN :], "dp", [(source, source + 1) for source in range(devices - 1)]
    )
    window = jnp.concatenate([halo, latents], axis=0)
    rope = window[:, KV_RANK:]
    blank = jnp.zeros((rows + MAXLEN, 2 * (128 - ROPE)), window.dtype)
    window = jnp.concatenate([window, blank, rope], axis=1)

    traces = lengths.shape[0]
    order = jnp.arange(traces, dtype=jnp.int32)
    ends = jnp.sum(jnp.where(order[None, :] <= order[:, None], lengths[None, :], 0), axis=1)
    first_row = device * rows
    position = first_row + jnp.arange(rows, dtype=jnp.int32)
    start = jnp.max(jnp.where(ends[None, :] <= position[:, None], ends[None, :], 0), axis=1)
    start = (start - first_row)[:, None]

    if devices * BLOCK == OUT_WIDTH:
        attn_out, hessian = fused(window, start, kv_weight, queries, devices, inverse_count)
        return attn_out, hessian
    attn_out = attention(window, start, kv_weight, queries)
    partial = lax.dot_general(
        attn_out, attn_out, (((0,), (0,)), ((), ())), preferred_element_type=jnp.float32
    )
    hessian = lax.psum_scatter(partial, "dp", scatter_dimension=0, tiled=True)
    return attn_out, hessian * inverse_count


def solution(mesh):
    placed = (P(("rep", "dp"), None), P(("rep", "dp"), None), P(), P("rep"))
    return jax.shard_map(
        per_device,
        mesh=mesh,
        in_specs=placed,
        out_specs=(P(("rep", "dp"), None), P(("rep", "dp"), None)),
        check_vma=False,
    )
```

time: 99.9 us -> 93.3 us (0.934)
  Pallas kernels: 83.1 us -> 79 us
  local copies, waits for them, and re-layouts: 8.96 us -> 5.94 us
    pallas_call x2 -> x1, Pallas kernels: 83.1 us -> 79 us  [fused(): pl.pallas_call(body, grid=(steps,), in_specs=[pl.BlockSpec(window.shape,...]
    unnamed x8 -> x5, local copies, waits for them, and re-layouts: 8.76 us -> 5.05 us
  transfers between devices with their start and end apart: 1 -> 1, of which waited for: 1 -> 1; matrix products, arithmetic and copies ran while one was open for 1% -> 2% of each run, Pallas kernels for 0% -> 0%
where the time goes in v2:
time: 93.3 us; the launch traced here: 92.6 us
  Pallas kernels  79 us (85%)
  local copies, waits for them, and re-layouts  5.94 us (6%)
  starting transfers between devices  4.54 us (5%)
  other arithmetic  1.94 us (2%)
    pallas_call x1, Pallas kernels, fused(): pl.pallas_call(body, grid=(steps,), in_specs=[pl.BlockSpec(window.shape,...  79 us
    unnamed x5, local copies, waits for them, and re-layouts  5.05 us
    ppermute x1, starting transfers between devices, per_device(): lax.ppermute(latents[rows - MAXLEN:], 'dp', [(source, source + 1) for sou...  4.54 us
  transfers between devices with their start and end apart: 1, of which 1 were waited for; matrix products, arithmetic and copies ran while one was open for 2% of the time, Pallas kernels for 0%

profile of v2, /device:TPU:1, one launch (start us, length us, event | category | flops | bytes accessed | tf_op | source)
XLA Modules:
  0.0 92.6 jit_solution(11411289234344179620)
XLA Ops:
  0.6 1.3 %copy.11 = bf16[384,576]{1,0:T(8,128)(2,1)S(1)} copy(bf16[384,576]{0,1:T(8,128)(2,1)} %param.5) | data formatting | bytes 884736 | tf_op args[1]
  1.9 4.5 %collective-permute-start = (bf16[128,576]{1,0:T(8,128)(2,1)S(1)}, bf16[128,576]{1,0:T(8,128)(2,1)S(1)}, u32[]{:S(2)}, u32[]{:S(2)}) collective-permute-start(bf16[128,576]{1,0:T(8,128)(2,1)S(1)} %slice.8), channel_id=1, source_target_pairs={{0,1},{1,2},{2,3},{3,4},{4,5},{5,6},{6,7},{7,8},{8,9},{9,10},{10,1... | collective-permute-start | bytes 442376 | tf_op jit(solution)/shard_map/ppermute | solution.py:315
  6.5 0.8 select_reduce_fusion.1
  7.2 0.1 select_reduce_fusion
  7.4 0.8 sub.16.refs_1_
  8.2 0.1 pad.2.clone
  8.2 0.5 collective-permute-done
  8.7 1.1 %fusion.3.refs_0_ = bf16[512,768]{1,0:T(8,128)(2,1)} fusion(bf16[384,576]{1,0:T(8,128)(2,1)S(1)} %copy.11, bf16[128,576]{1,0:T(8,128)(2,1)S(1)} %collective-permute-done, bf16[768]{0:T(1024)(128)(2,1)S(1)} %pad.2.clone), kind=kLoop, calls=%fused_computation.4 | loop fusion | flops 5111808 | bytes 1377792 | tf_op jit(solution)/shard_map/concatenate | solution.py:321
  9.8 79.0 %shard_map.59 = (bf16[384,2048]{1,0:T(8,128)(2,1)}, f32[128,2048]{1,0:T(8,128)}) custom-call(bf16[512,768]{1,0:T(8,128)(2,1)} %fusion.3.refs_0_, s32[384,1]{1,0:T(8,128)} %sub.16.refs_1_, bf16[512,6144]{1,0:T(8,128)(2,1)} %refs_2_.1, bf16[384,6144]{1,0:T(8,128)(2,1)} %refs_3_.1), custom_call_target="tpu_custom_call" | custom-call | tf_op jit(solution)/shard_map/pallas_call | solution.py:269
  88.8 0.0 copy-start
  88.8 2.8 %copy.16 = bf16[384,2048]{1,0:T(8,128)(2,1)} copy(bf16[384,2048]{1,0:T(8,128)(2,1)} %get-tuple-element.4) | data formatting | bytes 3145728
  91.6 0.0 copy-done
  91.6 1.0 %copy.17 = f32[128,2048]{1,0:T(8,128)} copy(f32[128,2048]{1,0:T(8,128)S(1)} %copy-done) | data formatting | bytes 2097152
  (4 shorter events, 0.0 us)
Async XLA Ops:
  1.9 6.8 %collective-permute-start = (bf16[128,576]{1,0:T(8,128)(2,1)S(1)}, bf16[128,576]{1,0:T(8,128)(2,1)S(1)}, u32[]{:S(2)}, u32[]{:S(2)}) collective-permute-start(bf16[128,576]{1,0:T(8,128)(2,1)S(1)} %slice.8), channel_id=1, source_target_pairs={{0,1},{1,2},{2,3},{3,4},{4,5},{5,6},{6,7},{7,8},{8,9},{9,10},{10,1... | collective-permute-start | bytes 442376 | tf_op jit(solution)/shard_map/ppermute | solution.py:315
  88.8 2.8 %copy-start = (f32[128,2048]{1,0:T(8,128)S(1)}, f32[128,2048]{1,0:T(8,128)}, u32[]{:S(2)}) copy-start(f32[128,2048]{1,0:T(8,128)} %get-tuple-element.5) | copy-start | bytes 3145732

commit v3 on v2

--- a/solution.py
+++ b/solution.py
@@ -19,9 +19,11 @@
 BLOCK = 128
 HEAD_WIDTH = NOPE + ROPE
 PAIR = 2 * HEAD_WIDTH
-PAIRS_PER_STEP = 2
+PAIRS_PER_STEP = 1
 STRIP = 9 * BLOCK
 LAG = 2
+HALVES = 2
+HALF = BLOCK // HALVES
 MESH = pl.DeviceIdType.MESH
 EXP_SCALE = math.log2(math.e) / math.sqrt(NOPE + ROPE)
 
@@ -114,6 +116,7 @@
     hessian_ref,
     bias_ref,
     a_all,
+    acc,
     z_send,
     z_recv,
     t_send,
@@ -132,7 +135,6 @@
     rows = query_ref.shape[0]
     width = out_ref.shape[1]
     steps = OUT_WIDTH // width
-    zs = devices // 4
     step = pl.program_id(0)
     me = lax.axis_index("dp")
     rep = lax.axis_index("rep")
@@ -192,41 +194,71 @@
 
     @pl.when(step == steps - 1)
     def _():
-        for piece in range(steps - LAG, steps):
-            y_copy(piece).wait_recv()
-            pass_copy(piece).start()
-        for piece in range(steps):
-            pair_copy(piece).wait_recv()
-            pass_copy(piece).wait_recv()
-        a_all[:, OUT_WIDTH:] = a_all[:, : STRIP - BLOCK]
-
-        def strip(owner):
+        z_low, z_high = lax.rem(z, 2), z // 2
+        beside = index_of(z_high * 2 + 1 - z_low, y, core)
+        beyond = index_of((1 - z_high) * 2 + z_low, y, core)
+        owners = (index_of((1 - z_high) * 2 + 1 - z_low, y, core), beside, beyond, me)
+
+        def strip(owner, first, last):
             at = pl.multiple_of(owner * BLOCK, BLOCK)
             return lax.dot_general(
-                a_all[:, pl.ds(at, BLOCK)],
-                a_all[:, pl.ds(at, STRIP)],
+                a_all[first * rows : last * rows, pl.ds(at, BLOCK)],
+                a_all[first * rows : last * rows, pl.ds(at, STRIP)],
                 (((0,), (0,)), ((), ())),
                 preferred_element_type=jnp.float32,
             )
 
-        z_copies = []
-        for j in range(zs - 1):
-            target = index_of(lax.rem(z + 1 + j, zs), y, core)
-            z_send[j] = strip(target).astype(jnp.bfloat16)
-            copy = pltpu.make_async_remote_copy(
-                src_ref=z_send.at[j],
-                dst_ref=z_recv.at[j],
-                send_sem=z_send_sem.at[j],
-                recv_sem=z_recv_sem.at[j],
-                device_id=(rep, target),
+        def wrap(first, last):
+            a_all[first * rows : last * rows, OUT_WIDTH:] = a_all[
+                first * rows : last * rows, : STRIP - BLOCK
+            ]
+
+        def z_copy(j, half, device):
+            at = slice(half * HALF, (half + 1) * HALF)
+            return pltpu.make_async_remote_copy(
+                src_ref=z_send.at[j, at],
+                dst_ref=z_recv.at[j, at],
+                send_sem=z_send_sem.at[j * HALVES + half],
+                recv_sem=z_recv_sem.at[j * HALVES + half],
+                device_id=(rep, device),
                 device_id_type=MESH,
             )
-            copy.start()
-            z_copies.append(copy)
-        total = strip(me)
-        for j in range(zs - 1):
-            z_copies[j].wait_recv()
-            total = total + z_recv[j].astype(jnp.float32)
+
+        def forward(piece):
+            y_copy(piece).wait_recv()
+            pass_copy(piece).start()
+
+        for piece in range(steps):
+            pair_copy(piece).wait_recv()
+        wrap(0, 2)
+        for j in range(4):
+            acc[j] = strip(owners[j], 0, 2)
+            if j % 2 == 1:
+                forward(steps - 2 + j // 2)
+        wrap(2, 3)
+        acc[0] = acc[0] + strip(owners[0], 2, 3)
+        for piece in range(steps):
+            pass_copy(piece).wait_recv()
+        wrap(3, 4)
+        z_send[0] = (acc[0] + strip(owners[0], 3, 4)).astype(jnp.bfloat16)
+        for half in range(HALVES):
+            z_copy(0, half, beside).start()
+        z_send[1] = (acc[1] + strip(owners[1], 2, 4)).astype(jnp.bfloat16)
+        for half in range(HALVES):
+            z_copy(1, half, beside).start()
+        acc[2] = acc[2] + strip(owners[2], 2, 4)
+        acc[3] = acc[3] + strip(owners[3], 2, 4)
+        for half in range(HALVES):
+            at = slice(half * HALF, (half + 1) * HALF)
+            z_copy(0, half, beside).wait_recv()
+            z_send[2, at] = (acc[2, at] + z_recv[0, at].astype(jnp.float32)).astype(jnp.bfloat16)
+            z_copy(2, half, beyond).start()
+        for half in range(HALVES):
+            z_copy(1, half, beside).wait_recv()
+        total = acc[3] + z_recv[1].astype(jnp.float32)
+        for half in range(HALVES):
+            z_copy(2, half, beyond).wait_recv()
+        total = total + z_recv[2].astype(jnp.float32)
         total = total * inverse_count
 
         t_copies = []
@@ -253,7 +285,11 @@
             pair_copy(piece).wait_send()
             y_copy(piece).wait_send()
             pass_copy(piece).wait_send()
-        for copy in z_copies + t_copies:
+        for half in range(HALVES):
+            z_copy(0, half, beside).wait_send()
+            z_copy(1, half, beside).wait_send()
+            z_copy(2, half, beyond).wait_send()
+        for copy in t_copies:
             copy.wait_send()
 
 
@@ -261,7 +297,6 @@
     rows = queries.shape[0]
     span = PAIR * PAIRS_PER_STEP
     steps = queries.shape[1] // span
-    zs = devices // 4
 
     def body(*refs):
         fused_kernel(devices, inverse_count, *refs)
@@ -286,8 +321,9 @@
         scratch_shapes=[
             pltpu.VMEM((rows, 2 * BLOCK), jnp.float32),
             pltpu.VMEM((4 * rows, OUT_WIDTH + STRIP - BLOCK), jnp.bfloat16),
-            pltpu.VMEM((zs - 1, BLOCK, STRIP), jnp.bfloat16),
-            pltpu.VMEM((zs - 1, BLOCK, STRIP), jnp.bfloat16),
+            pltpu.VMEM((4, BLOCK, STRIP), jnp.float32),
+            pltpu.VMEM((3, BLOCK, STRIP), jnp.bfloat16),
+            pltpu.VMEM((3, BLOCK, STRIP), jnp.bfloat16),
             pltpu.VMEM((7, BLOCK, BLOCK), jnp.bfloat16),
             pltpu.VMEM((7, BLOCK, BLOCK), jnp.bfloat16),
             pltpu.SemaphoreType.DMA((steps,)),
@@ -296,8 +332,8 @@
             pltpu.SemaphoreType.DMA((steps,)),
             pltpu.SemaphoreType.DMA((steps,)),
             pltpu.SemaphoreType.DMA((steps,)),
-            pltpu.SemaphoreType.DMA((zs - 1,)),
-            pltpu.SemaphoreType.DMA((zs - 1,)),
+            pltpu.SemaphoreType.DMA((3 * HALVES,)),
+            pltpu.SemaphoreType.DMA((3 * HALVES,)),
             pltpu.SemaphoreType.DMA((7,)),
             pltpu.SemaphoreType.DMA((7,)),
         ],
@@ -328,7 +364,7 @@
     start = jnp.max(jnp.where(ends[None, :] <= position[:, None], ends[None, :], 0), axis=1)
     start = (start - first_row)[:, None]
 
-    if devices * BLOCK == OUT_WIDTH:
+    if devices == 16:
         attn_out, hessian = fused(window, start, kv_weight, queries, devices, inverse_count)
         return attn_out, hessian
     attn_out = attention(window, start, kv_weight, queries)

time: 93.3 us -> 89.2 us (0.956)
  Pallas kernels: 79 us -> 75.4 us
    pallas_call x1, Pallas kernels: 79 us -> 75.4 us  [fused(): pl.pallas_call(body, grid=(steps,), in_specs=[pl.BlockSpec(window.shape,...]
where the time goes in v3:
time: 89.2 us; the launch traced here: 88.9 us
  Pallas kernels  75.4 us (85%)
  local copies, waits for them, and re-layouts  5.94 us (7%)
  starting transfers between devices  4.54 us (5%)
  other arithmetic  1.94 us (2%)
    pallas_call x1, Pallas kernels, fused(): pl.pallas_call(body, grid=(steps,), in_specs=[pl.BlockSpec(window.shape,...  75.4 us
    unnamed x5, local copies, waits for them, and re-layouts  5.05 us
    ppermute x1, starting transfers between devices, per_device(): lax.ppermute(latents[rows - MAXLEN:], 'dp', [(source, source + 1) for sou...  4.54 us
  transfers between devices with their start and end apart: 1, of which 1 were waited for; matrix products, arithmetic and copies ran while one was open for 2% of the time, Pallas kernels for 0%

profile of v3, /device:TPU:1, one launch (start us, length us, event | category | flops | bytes accessed | tf_op | source)
XLA Modules:
  0.0 88.9 jit_solution(13092652354254003633)
XLA Ops:
  0.6 1.3 %copy.11 = bf16[384,576]{1,0:T(8,128)(2,1)S(1)} copy(bf16[384,576]{0,1:T(8,128)(2,1)} %param.5) | data formatting | bytes 884736 | tf_op args[1]
  1.9 4.5 %collective-permute-start = (bf16[128,576]{1,0:T(8,128)(2,1)S(1)}, bf16[128,576]{1,0:T(8,128)(2,1)S(1)}, u32[]{:S(2)}, u32[]{:S(2)}) collective-permute-start(bf16[128,576]{1,0:T(8,128)(2,1)S(1)} %slice.8), channel_id=1, source_target_pairs={{0,1},{1,2},{2,3},{3,4},{4,5},{5,6},{6,7},{7,8},{8,9},{9,10},{10,1... | collective-permute-start | bytes 442376 | tf_op jit(solution)/shard_map/ppermute | solution.py:351
  6.5 0.8 select_reduce_fusion.1
  7.2 0.1 select_reduce_fusion
  7.4 0.8 sub.16.refs_1_
  8.2 0.1 pad.2.clone
  8.2 0.5 collective-permute-done
  8.7 1.1 %fusion.3.refs_0_ = bf16[512,768]{1,0:T(8,128)(2,1)} fusion(bf16[384,576]{1,0:T(8,128)(2,1)S(1)} %copy.11, bf16[128,576]{1,0:T(8,128)(2,1)S(1)} %collective-permute-done, bf16[768]{0:T(1024)(128)(2,1)S(1)} %pad.2.clone), kind=kLoop, calls=%fused_computation.4 | loop fusion | flops 5111808 | bytes 1377792 | tf_op jit(solution)/shard_map/concatenate | solution.py:357
  9.8 75.4 %shard_map.59 = (bf16[384,2048]{1,0:T(8,128)(2,1)}, f32[128,2048]{1,0:T(8,128)}) custom-call(bf16[512,768]{1,0:T(8,128)(2,1)} %fusion.3.refs_0_, s32[384,1]{1,0:T(8,128)} %sub.16.refs_1_, bf16[512,6144]{1,0:T(8,128)(2,1)} %refs_2_.1, bf16[384,6144]{1,0:T(8,128)(2,1)} %refs_3_.1), custom_call_target="tpu_custom_call" | custom-call | tf_op jit(solution)/shard_map/pallas_call | solution.py:304
  85.1 0.0 copy-start
  85.2 2.8 %copy.16 = bf16[384,2048]{1,0:T(8,128)(2,1)} copy(bf16[384,2048]{1,0:T(8,128)(2,1)} %get-tuple-element.4) | data formatting | bytes 3145728
  88.0 0.0 copy-done
  88.0 1.0 %copy.17 = f32[128,2048]{1,0:T(8,128)} copy(f32[128,2048]{1,0:T(8,128)S(1)} %copy-done) | data formatting | bytes 2097152
  (4 shorter events, 0.0 us)
Async XLA Ops:
  1.9 6.8 %collective-permute-start = (bf16[128,576]{1,0:T(8,128)(2,1)S(1)}, bf16[128,576]{1,0:T(8,128)(2,1)S(1)}, u32[]{:S(2)}, u32[]{:S(2)}) collective-permute-start(bf16[128,576]{1,0:T(8,128)(2,1)S(1)} %slice.8), channel_id=1, source_target_pairs={{0,1},{1,2},{2,3},{3,4},{4,5},{5,6},{6,7},{7,8},{8,9},{9,10},{10,1... | collective-permute-start | bytes 442376 | tf_op jit(solution)/shard_map/ppermute | solution.py:351
  85.1 2.8 %copy-start = (f32[128,2048]{1,0:T(8,128)S(1)}, f32[128,2048]{1,0:T(8,128)}, u32[]{:S(2)}) copy-start(f32[128,2048]{1,0:T(8,128)} %get-tuple-element.5) | copy-start | bytes 3145732

commit v4 on v3

--- a/solution.py
+++ b/solution.py
@@ -23,7 +23,7 @@
 STRIP = 9 * BLOCK
 LAG = 2
 HALVES = 2
-HALF = BLOCK // HALVES
+CUTS = (0, 5 * BLOCK, STRIP)
 MESH = pl.DeviceIdType.MESH
 EXP_SCALE = math.log2(math.e) / math.sqrt(NOPE + ROPE)
 
@@ -214,10 +214,10 @@
             ]
 
         def z_copy(j, half, device):
-            at = slice(half * HALF, (half + 1) * HALF)
+            at = slice(CUTS[half], CUTS[half + 1])
             return pltpu.make_async_remote_copy(
-                src_ref=z_send.at[j, at],
-                dst_ref=z_recv.at[j, at],
+                src_ref=z_send.at[j, :, at],
+                dst_ref=z_recv.at[j, :, at],
                 send_sem=z_send_sem.at[j * HALVES + half],
                 recv_sem=z_recv_sem.at[j * HALVES + half],
                 device_id=(rep, device),
@@ -249,34 +249,32 @@
         acc[2] = acc[2] + strip(owners[2], 2, 4)
         acc[3] = acc[3] + strip(owners[3], 2, 4)
         for half in range(HALVES):
-            at = slice(half * HALF, (half + 1) * HALF)
+            at = slice(CUTS[half], CUTS[half + 1])
             z_copy(0, half, beside).wait_recv()
-            z_send[2, at] = (acc[2, at] + z_recv[0, at].astype(jnp.float32)).astype(jnp.bfloat16)
+            z_send[2, :, at] = (acc[2, :, at] + z_recv[0, :, at].astype(jnp.float32)).astype(jnp.bfloat16)
             z_copy(2, half, beyond).start()
-        for half in range(HALVES):
+        t_copies = []
+        for half in range(HALVES):
+            at = slice(CUTS[half], CUTS[half + 1])
             z_copy(1, half, beside).wait_recv()
-        total = acc[3] + z_recv[1].astype(jnp.float32)
-        for half in range(HALVES):
+            total = acc[3, :, at] + z_recv[1, :, at].astype(jnp.float32)
             z_copy(2, half, beyond).wait_recv()
-        total = total + z_recv[2].astype(jnp.float32)
-        total = total * inverse_count
-
-        t_copies = []
-        for k in range(1, 8):
-            t_send[k - 1] = total[:, k * BLOCK : (k + 1) * BLOCK].T.astype(jnp.bfloat16)
-            copy = pltpu.make_async_remote_copy(
-                src_ref=t_send.at[k - 1],
-                dst_ref=t_recv.at[k - 1],
-                send_sem=t_send_sem.at[k - 1],
-                recv_sem=t_recv_sem.at[k - 1],
-                device_id=(rep, other(k)),
-                device_id_type=MESH,
-            )
-            copy.start()
-            t_copies.append(copy)
+            acc[3, :, at] = (total + z_recv[2, :, at].astype(jnp.float32)) * inverse_count
+            for k in range(max(1, CUTS[half] // BLOCK), min(8, CUTS[half + 1] // BLOCK)):
+                t_send[k - 1] = acc[3, :, k * BLOCK : (k + 1) * BLOCK].T.astype(jnp.bfloat16)
+                copy = pltpu.make_async_remote_copy(
+                    src_ref=t_send.at[k - 1],
+                    dst_ref=t_recv.at[k - 1],
+                    send_sem=t_send_sem.at[k - 1],
+                    recv_sem=t_recv_sem.at[k - 1],
+                    device_id=(rep, other(k)),
+                    device_id_type=MESH,
+                )
+                copy.start()
+                t_copies.append(copy)
         for k in range(9):
             at = pl.multiple_of(other(k) * BLOCK, BLOCK)
-            hessian_ref[:, pl.ds(at, BLOCK)] = total[:, k * BLOCK : (k + 1) * BLOCK]
+            hessian_ref[:, pl.ds(at, BLOCK)] = acc[3, :, k * BLOCK : (k + 1) * BLOCK]
         for k in range(1, 8):
             t_copies[k - 1].wait_recv()
             at = pl.multiple_of(other(devices - k) * BLOCK, BLOCK)

time: 89.2 us -> 88.4 us (level)
  no operation moved by 1% of the time
where the time goes in v4:
time: 88.4 us; the launch traced here: 88.1 us
  Pallas kernels  74.6 us (84%)
  local copies, waits for them, and re-layouts  5.94 us (7%)
  starting transfers between devices  4.54 us (5%)
  other arithmetic  1.94 us (2%)
    pallas_call x1, Pallas kernels, fused(): pl.pallas_call(body, grid=(steps,), in_specs=[pl.BlockSpec(window.shape,...  74.6 us
    unnamed x5, local copies, waits for them, and re-layouts  5.05 us
    ppermute x1, starting transfers between devices, per_device(): lax.ppermute(latents[rows - MAXLEN:], 'dp', [(source, source + 1) for sou...  4.54 us
  transfers between devices with their start and end apart: 1, of which 1 were waited for; matrix products, arithmetic and copies ran while one was open for 2% of the time, Pallas kernels for 0%

profile of v4, /device:TPU:1, one launch (start us, length us, event | category | flops | bytes accessed | tf_op | source)
XLA Modules:
  0.0 88.1 jit_solution(10507870974157154258)
XLA Ops:
  0.6 1.3 %copy.11 = bf16[384,576]{1,0:T(8,128)(2,1)S(1)} copy(bf16[384,576]{0,1:T(8,128)(2,1)} %param.5) | data formatting | bytes 884736 | tf_op args[1]
  1.9 4.5 %collective-permute-start = (bf16[128,576]{1,0:T(8,128)(2,1)S(1)}, bf16[128,576]{1,0:T(8,128)(2,1)S(1)}, u32[]{:S(2)}, u32[]{:S(2)}) collective-permute-start(bf16[128,576]{1,0:T(8,128)(2,1)S(1)} %slice.8), channel_id=1, source_target_pairs={{0,1},{1,2},{2,3},{3,4},{4,5},{5,6},{6,7},{7,8},{8,9},{9,10},{10,1... | collective-permute-start | bytes 442376 | tf_op jit(solution)/shard_map/ppermute | solution.py:349
  6.5 0.8 select_reduce_fusion.1
  7.2 0.1 select_reduce_fusion
  7.4 0.8 sub.16.refs_1_
  8.2 0.1 pad.2.clone
  8.2 0.5 collective-permute-done
  8.7 1.1 %fusion.3.refs_0_ = bf16[512,768]{1,0:T(8,128)(2,1)} fusion(bf16[384,576]{1,0:T(8,128)(2,1)S(1)} %copy.11, bf16[128,576]{1,0:T(8,128)(2,1)S(1)} %collective-permute-done, bf16[768]{0:T(1024)(128)(2,1)S(1)} %pad.2.clone), kind=kLoop, calls=%fused_computation.4 | loop fusion | flops 5111808 | bytes 1377792 | tf_op jit(solution)/shard_map/concatenate | solution.py:355
  9.8 74.6 %shard_map.59 = (bf16[384,2048]{1,0:T(8,128)(2,1)}, f32[128,2048]{1,0:T(8,128)}) custom-call(bf16[512,768]{1,0:T(8,128)(2,1)} %fusion.3.refs_0_, s32[384,1]{1,0:T(8,128)} %sub.16.refs_1_, bf16[512,6144]{1,0:T(8,128)(2,1)} %refs_2_.1, bf16[384,6144]{1,0:T(8,128)(2,1)} %refs_3_.1), custom_call_target="tpu_custom_call" | custom-call | tf_op jit(solution)/shard_map/pallas_call | solution.py:302
  84.3 0.0 copy-start
  84.4 2.8 %copy.16 = bf16[384,2048]{1,0:T(8,128)(2,1)} copy(bf16[384,2048]{1,0:T(8,128)(2,1)} %get-tuple-element.4) | data formatting | bytes 3145728
  87.2 0.0 copy-done
  87.2 1.0 %copy.17 = f32[128,2048]{1,0:T(8,128)} copy(f32[128,2048]{1,0:T(8,128)S(1)} %copy-done) | data formatting | bytes 2097152
  (4 shorter events, 0.0 us)
Async XLA Ops:
  1.9 6.8 %collective-permute-start = (bf16[128,576]{1,0:T(8,128)(2,1)S(1)}, bf16[128,576]{1,0:T(8,128)(2,1)S(1)}, u32[]{:S(2)}, u32[]{:S(2)}) collective-permute-start(bf16[128,576]{1,0:T(8,128)(2,1)S(1)} %slice.8), channel_id=1, source_target_pairs={{0,1},{1,2},{2,3},{3,4},{4,5},{5,6},{6,7},{7,8},{8,9},{9,10},{10,1... | collective-permute-start | bytes 442376 | tf_op jit(solution)/shard_map/ppermute | solution.py:349
  84.3 2.8 %copy-start = (f32[128,2048]{1,0:T(8,128)S(1)}, f32[128,2048]{1,0:T(8,128)}, u32[]{:S(2)}) copy-start(f32[128,2048]{1,0:T(8,128)} %get-tuple-element.5) | copy-start | bytes 3145732

commit v5 on v4

--- a/solution.py
+++ b/solution.py
@@ -22,8 +22,8 @@
 PAIRS_PER_STEP = 1
 STRIP = 9 * BLOCK
 LAG = 2
-HALVES = 2
-CUTS = (0, 5 * BLOCK, STRIP)
+HALVES = 3
+CUTS = (0, 3 * BLOCK, 6 * BLOCK, STRIP)
 MESH = pl.DeviceIdType.MESH
 EXP_SCALE = math.log2(math.e) / math.sqrt(NOPE + ROPE)
 

time: 88.4 us -> 88.5 us (level)
  no operation moved by 1% of the time
where the time goes in v5:
time: 88.5 us; the launch traced here: 88.2 us
  Pallas kernels  74.7 us (84%)
  local copies, waits for them, and re-layouts  5.94 us (7%)
  starting transfers between devices  4.54 us (5%)
  other arithmetic  1.94 us (2%)
    pallas_call x1, Pallas kernels, fused(): pl.pallas_call(body, grid=(steps,), in_specs=[pl.BlockSpec(window.shape,...  74.7 us
    unnamed x5, local copies, waits for them, and re-layouts  5.05 us
    ppermute x1, starting transfers between devices, per_device(): lax.ppermute(latents[rows - MAXLEN:], 'dp', [(source, source + 1) for sou...  4.54 us
  transfers between devices with their start and end apart: 1, of which 1 were waited for; matrix products, arithmetic and copies ran while one was open for 2% of the time, Pallas kernels for 0%

profile of v5, /device:TPU:1, one launch (start us, length us, event | category | flops | bytes accessed | tf_op | source)
XLA Modules:
  0.0 88.2 jit_solution(12578076806618731199)
XLA Ops:
  0.6 1.3 %copy.11 = bf16[384,576]{1,0:T(8,128)(2,1)S(1)} copy(bf16[384,576]{0,1:T(8,128)(2,1)} %param.5) | data formatting | bytes 884736 | tf_op args[1]
  1.9 4.5 %collective-permute-start = (bf16[128,576]{1,0:T(8,128)(2,1)S(1)}, bf16[128,576]{1,0:T(8,128)(2,1)S(1)}, u32[]{:S(2)}, u32[]{:S(2)}) collective-permute-start(bf16[128,576]{1,0:T(8,128)(2,1)S(1)} %slice.8), channel_id=1, source_target_pairs={{0,1},{1,2},{2,3},{3,4},{4,5},{5,6},{6,7},{7,8},{8,9},{9,10},{10,1... | collective-permute-start | bytes 442376 | tf_op jit(solution)/shard_map/ppermute | solution.py:349
  6.5 0.8 select_reduce_fusion.1
  7.2 0.1 select_reduce_fusion
  7.4 0.8 sub.16.refs_1_
  8.2 0.1 pad.2.clone
  8.2 0.5 collective-permute-done
  8.7 1.1 %fusion.3.refs_0_ = bf16[512,768]{1,0:T(8,128)(2,1)} fusion(bf16[384,576]{1,0:T(8,128)(2,1)S(1)} %copy.11, bf16[128,576]{1,0:T(8,128)(2,1)S(1)} %collective-permute-done, bf16[768]{0:T(1024)(128)(2,1)S(1)} %pad.2.clone), kind=kLoop, calls=%fused_computation.4 | loop fusion | flops 5111808 | bytes 1377792 | tf_op jit(solution)/shard_map/concatenate | solution.py:355
  9.8 74.7 %shard_map.59 = (bf16[384,2048]{1,0:T(8,128)(2,1)}, f32[128,2048]{1,0:T(8,128)}) custom-call(bf16[512,768]{1,0:T(8,128)(2,1)} %fusion.3.refs_0_, s32[384,1]{1,0:T(8,128)} %sub.16.refs_1_, bf16[512,6144]{1,0:T(8,128)(2,1)} %refs_2_.1, bf16[384,6144]{1,0:T(8,128)(2,1)} %refs_3_.1), custom_call_target="tpu_custom_call" | custom-call | tf_op jit(solution)/shard_map/pallas_call | solution.py:302
  84.4 0.0 copy-start
  84.5 2.8 %copy.16 = bf16[384,2048]{1,0:T(8,128)(2,1)} copy(bf16[384,2048]{1,0:T(8,128)(2,1)} %get-tuple-element.4) | data formatting | bytes 3145728
  87.3 0.0 copy-done
  87.3 1.0 %copy.17 = f32[128,2048]{1,0:T(8,128)} copy(f32[128,2048]{1,0:T(8,128)S(1)} %copy-done) | data formatting | bytes 2097152
  (4 shorter events, 0.0 us)
Async XLA Ops:
  1.9 6.8 %collective-permute-start = (bf16[128,576]{1,0:T(8,128)(2,1)S(1)}, bf16[128,576]{1,0:T(8,128)(2,1)S(1)}, u32[]{:S(2)}, u32[]{:S(2)}) collective-permute-start(bf16[128,576]{1,0:T(8,128)(2,1)S(1)} %slice.8), channel_id=1, source_target_pairs={{0,1},{1,2},{2,3},{3,4},{4,5},{5,6},{6,7},{7,8},{8,9},{9,10},{10,1... | collective-permute-start | bytes 442376 | tf_op jit(solution)/shard_map/ppermute | solution.py:349
  84.4 2.8 %copy-start = (f32[128,2048]{1,0:T(8,128)S(1)}, f32[128,2048]{1,0:T(8,128)}, u32[]{:S(2)}) copy-start(f32[128,2048]{1,0:T(8,128)} %get-tuple-element.5) | copy-start | bytes 3145732
